TPU v7x, 32 devices: a whole 2x2x4 slice. The times are simulated.
32 devices in a mesh: dp: 8 (over z, y), mp: 4 (over x, core).
Axes of the slice: x: 2, y: 2, z: 4, core: 2. Of those that a mesh axis runs over, the one named last changes fastest.
Arguments:
- tokens: bfloat16 [8192, 1152], P('dp'), may hold values from -6 to 6
- timesteps: int32 [32], P('dp'), may hold values from 0 to 999
- relative_index: int32 [256, 256], replicated, may hold values from 0 to 960, as said below
- time_table: bfloat16 [1000, 1152], replicated, may hold values from -6 to 6
- query_weight: bfloat16 [1152, 1152], replicated, may hold values from -0.1875 to 0.1875
- key_weight: bfloat16 [1152, 1152], replicated, may hold values from -0.1875 to 0.1875
- value_weight: bfloat16 [1152, 1152], replicated, may hold values from -0.1875 to 0.1875
- time_query_weight: bfloat16 [1152, 1152], replicated, may hold values from -0.1875 to 0.1875
- time_value_weight: bfloat16 [1152, 1152], replicated, may hold values from -0.09375 to 0.09375
- out_weight: bfloat16 [1152, 1152], replicated, may hold values from -0.5 to 0.5
- out_bias: float32 [1152], replicated, may hold values from -3 to 3
- first_gain: float32 [1152], replicated, may hold values from 0.5 to 1.5
- first_shift: float32 [1152], replicated, may hold values from -3 to 3
- second_gain: float32 [1152], replicated, may hold values from 0.5 to 1.5
- second_shift: float32 [1152], replicated, may hold values from -3 to 3
- up_weight: bfloat16 [1152, 4608], P(None, 'mp'), may hold values from -0.1875 to 0.1875
- up_bias: float32 [4608], P('mp'), may hold values from -3 to 3
- down_weight: bfloat16 [4608, 1152], P('mp'), may hold values from -0.09375 to 0.09375
- down_bias: float32 [1152], replicated, may hold values from -3 to 3
- bias_table: float32 [961, 16], replicated, may hold values from -4 to 4
- cotangent: bfloat16 [8192, 1152], P(('dp', 'mp')), may hold values from -6 to 6
Outputs:
- block_out: bfloat16 [8192, 1152], P(('dp', 'mp'))
- tokens_grad: float32 [8192, 1152], P(('dp', 'mp'))
- time_table_grad: float32 [1000, 1152], P(None, 'mp')
- query_weight_grad: float32 [1152, 1152], P(None, 'mp')
- key_weight_grad: float32 [1152, 1152], P(None, 'mp')
- value_weight_grad: float32 [1152, 1152], P(None, 'mp')
- time_query_grad: float32 [1152, 1152], P(None, 'mp')
- time_value_grad: float32 [1152, 1152], P(None, 'mp')
- out_weight_grad: float32 [1152, 1152], P('mp')
- out_bias_grad: float32 [1152], P('mp')
- first_gain_grad: float32 [1152], P('mp')
- first_shift_grad: float32 [1152], P('mp')
- second_gain_grad: float32 [1152], P('mp')
- second_shift_grad: float32 [1152], P('mp')
- up_weight_grad: float32 [1152, 4608], P(None, 'mp')
- up_bias_grad: float32 [4608], P('mp')
- down_weight_grad: float32 [4608, 1152], P('mp')
- down_bias_grad: float32 [1152], P('mp')
- bias_table_grad: float32 [961, 16], P(None, 'mp')
Inputs may be any that keep to these rules, and one draw needn't show every extreme that they name: `relative_index`: the tokens of an image sit on distinct cells of a 16 x 16 grid; entry (i, j) is (row_i - row_j + 15) * 31 + column_i - column_j + 15.
All inputs are finite; a program needn't handle non-finite values.
Results may differ from a plain program's by a relative error of at most 0.013.
Values may be sent and summed in bfloat16 or wider, within the bound.
No kernel may reach another device: no remote copies, remote signals or barrier semaphores. Data moves between devices by JAX's collectives and lax.ppermute only.
A program may use at most 256 MiB of HBM per device.

v0:
```python
from functools import partial
import math

import jax
import jax.numpy as jnp
from jax import lax
from jax.sharding import PartitionSpec as P

EPSILON = 1e-06
HIGHEST = lax.Precision.HIGHEST


def norm_forward(values, gain_row, shift_row):
    average = jnp.mean(values, axis=-1, keepdims=True)
    centred = values - average
    inverse = lax.rsqrt(jnp.mean(centred * centred, axis=-1, keepdims=True) + EPSILON)
    unit_rows = centred * inverse
    return (unit_rows * gain_row + shift_row, unit_rows, inverse)


def norm_backward(grad_out, unit_rows, inverse, gain_row):
    grad_unit = grad_out * gain_row
    first_mean = jnp.mean(grad_unit, axis=-1, keepdims=True)
    second_mean = jnp.mean(grad_unit * unit_rows, axis=-1, keepdims=True)
    grad_in = inverse * (grad_unit - first_mean - unit_rows * second_mean)
    return (grad_in, jnp.sum(grad_out * unit_rows, axis=0), jnp.sum(grad_out, axis=0))


def attend_forward(query_rows, key_rows, value_rows, bias_full, score_scale):
    scores = (
        jnp.einsum("gqhe,gkhe->ghqk", query_rows, key_rows, preferred_element_type=jnp.float32)
        * score_scale
        + bias_full[None]
    )
    row_top = jnp.max(scores, axis=-1, keepdims=True)
    weights = jnp.exp(scores - row_top)
    totals = jnp.sum(weights, axis=-1, keepdims=True)
    probabilities = (weights / totals).astype(jnp.bfloat16)
    mixed = jnp.einsum(
        "ghqk,gkhe->gqhe", probabilities, value_rows, preferred_element_type=jnp.float32
    )
    return (mixed.astype(jnp.bfloat16), row_top + jnp.log(totals))


def attend_backward(
    query_rows, key_rows, value_rows, grad_mixed, log_total, bias_full, score_scale
):
    scores = (
        jnp.einsum("gqhe,gkhe->ghqk", query_rows, key_rows, preferred_element_type=jnp.float32)
        * score_scale
        + bias_full[None]
    )
    probabilities = jnp.exp(scores - log_total)
    grad_probs = jnp.einsum(
        "gqhe,gkhe->ghqk", grad_mixed, value_rows, preferred_element_type=jnp.float32
    )
    row_dot = jnp.sum(probabilities * grad_probs, axis=-1, keepdims=True)
    grad_scores = (probabilities * (grad_probs - row_dot)).astype(jnp.bfloat16)
    query_back = (
        jnp.einsum("ghqk,gkhe->gqhe", grad_scores, key_rows, preferred_element_type=jnp.float32)
        * score_scale
    ).astype(jnp.bfloat16)
    key_back = (
        jnp.einsum("ghqk,gqhe->gkhe", grad_scores, query_rows, preferred_element_type=jnp.float32)
        * score_scale
    ).astype(jnp.bfloat16)
    value_back = jnp.einsum(
        "ghqk,gqhe->gkhe",
        probabilities.astype(jnp.bfloat16),
        grad_mixed,
        preferred_element_type=jnp.float32,
    ).astype(jnp.bfloat16)
    return (query_back, key_back, value_back, jnp.sum(grad_scores.astype(jnp.float32), axis=0))


def padded_vector(arrays, devices):
    flat_vector = jnp.concatenate([member.reshape(-1) for member in arrays])
    return jnp.pad(flat_vector, (0, -flat_vector.shape[0] % devices))


def restore_all(flat_vector, layouts):
    results = []
    offset = 0
    for layout in layouts:
        extent = math.prod(layout)
        results.append(flat_vector[offset : offset + extent].reshape(layout))
        offset += extent
    return results


def reduce_all(arrays):
    summed = lax.psum_scatter(
        padded_vector(arrays, lax.axis_size("dp")), "dp", scatter_dimension=0, tiled=True
    )
    whole = lax.all_gather(summed, "dp", axis=0, tiled=True)
    return restore_all(whole, [member.shape for member in arrays])


def on_device(
    tokens,
    timesteps,
    relative_index,
    time_table,
    query_weight,
    key_weight,
    value_weight,
    time_query_weight,
    time_value_weight,
    out_weight,
    out_bias,
    first_gain,
    first_shift,
    second_gain,
    second_shift,
    up_weight,
    up_bias,
    down_weight,
    down_bias,
    bias_table,
    cotangent,
):
    images = timesteps.shape[0]
    token_rows = tokens.shape[0]
    length = token_rows // images
    model_width = tokens.shape[1]
    head_count = bias_table.shape[1]
    head_width = model_width // head_count
    model_size = lax.axis_size("mp")
    model_rank = lax.axis_index("mp")
    own_rows = token_rows // model_size
    row_start = model_rank * own_rows
    score_scale = head_width ** (-0.5)
    group_size = math.gcd(images, max(1, 512 // length))
    onehot = timesteps[:, None] == jnp.arange(time_table.shape[0], dtype=jnp.int32)[None, :]
    embedding = jnp.dot(
        onehot.astype(jnp.bfloat16), time_table, preferred_element_type=jnp.float32
    ).astype(jnp.bfloat16)
    tokens_wide = tokens.astype(jnp.float32)
    normed_first, unit_first, inverse_first = norm_forward(tokens_wide, first_gain, first_shift)
    normed_first = normed_first.astype(jnp.bfloat16)
    time_query = jnp.dot(embedding, time_query_weight, preferred_element_type=jnp.float32)
    time_value = jnp.dot(embedding, time_value_weight, preferred_element_type=jnp.float32)

    def project(matrix, extra):
        product = jnp.dot(normed_first, matrix, preferred_element_type=jnp.float32).reshape(
            images, length, -1
        )
        rounded = (product + extra[:, None, :]).astype(jnp.bfloat16)
        return rounded.reshape(images // group_size, group_size, length, head_count, head_width)

    query_rows = project(query_weight, time_query)
    key_rows = project(key_weight, jnp.zeros_like(time_query))
    value_rows = project(value_weight, time_value)
    bias_full = jnp.transpose(jnp.take(bias_table, relative_index, axis=0), (2, 0, 1))

    def forward_block(block_rows):
        return attend_forward(block_rows[0], block_rows[1], block_rows[2], bias_full, score_scale)

    mixed_rows, log_totals = lax.map(forward_block, (query_rows, key_rows, value_rows))
    mixed_flat = mixed_rows.reshape(token_rows, head_count * head_width)
    branch = jnp.dot(mixed_flat, out_weight, preferred_element_type=jnp.float32)
    middle = tokens_wide + branch + out_bias
    normed_second, unit_second, inverse_second = norm_forward(middle, second_gain, second_shift)
    normed_second = normed_second.astype(jnp.bfloat16)
    hidden = jnp.dot(normed_second, up_weight, preferred_element_type=jnp.float32) + up_bias
    gelu_out, gelu_back = jax.vjp(partial(jax.nn.gelu, approximate=True), hidden)
    active = gelu_out.astype(jnp.bfloat16)
    parts_sum = lax.psum_scatter(
        jnp.dot(
            lax.slice_in_dim(active, 0, own_rows * lax.axis_size("mp"), axis=0),
            down_weight,
            preferred_element_type=jnp.float32,
        ).astype(jnp.bfloat16),
        "mp",
        scatter_dimension=0,
        tiled=True,
    ).astype(jnp.float32)
    block_out = (
        lax.dynamic_slice_in_dim(middle, row_start, own_rows, 0) + parts_sum + down_bias
    ).astype(jnp.bfloat16)
    grad_full = lax.all_gather(cotangent, "mp", axis=0, tiled=True)
    grad_wide = grad_full.astype(jnp.float32)
    down_grad = jnp.einsum("rf,rd->fd", active, grad_full, preferred_element_type=jnp.float32)
    down_bias_grad = jnp.sum(grad_wide, axis=0)
    grad_active = jnp.einsum(
        "rd,fd->rf", grad_full, down_weight, preferred_element_type=jnp.float32
    )
    grad_hidden = gelu_back(grad_active)[0].astype(jnp.bfloat16)
    up_grad = jnp.einsum(
        "rd,rf->df", normed_second, grad_hidden, preferred_element_type=jnp.float32
    )
    up_bias_grad = jnp.sum(grad_hidden.astype(jnp.float32), axis=0)
    grad_normed_part = jnp.einsum(
        "rf,df->rd", grad_hidden, up_weight, preferred_element_type=jnp.float32
    )
    grad_normed = lax.psum(grad_normed_part, "mp")
    grad_mid_norm, second_gain_grad, second_shift_grad = norm_backward(
        grad_normed, unit_second, inverse_second, second_gain
    )
    grad_middle = grad_wide + grad_mid_norm
    out_bias_grad = jnp.sum(grad_middle, axis=0)
    grad_branch = grad_middle.astype(jnp.bfloat16)
    out_grad = jnp.einsum("ra,rd->ad", mixed_flat, grad_branch, preferred_element_type=jnp.float32)
    grad_mixed = jnp.einsum(
        "rd,ad->ra", grad_branch, out_weight, preferred_element_type=jnp.float32
    ).astype(jnp.bfloat16)
    grad_mixed = grad_mixed.reshape(
        images // group_size, group_size, length, head_count, head_width
    )

    def backward_block(running, block_rows):
        query_back, key_back, value_back, score_back = attend_backward(
            block_rows[0],
            block_rows[1],
            block_rows[2],
            block_rows[3],
            block_rows[4],
            bias_full,
            score_scale,
        )
        return (running + score_back, (query_back, key_back, value_back))

    score_total, (grad_query, grad_key, grad_value) = lax.scan(
        backward_block,
        jnp.zeros((head_count, length, length), jnp.float32),
        (query_rows, key_rows, value_rows, grad_mixed, log_totals),
    )
    flat_query = grad_query.reshape(token_rows, head_count * head_width)
    flat_key = grad_key.reshape(token_rows, head_count * head_width)
    flat_value = grad_value.reshape(token_rows, head_count * head_width)
    query_grad = jnp.einsum(
        "rd,ra->da", normed_first, flat_query, preferred_element_type=jnp.float32
    )
    key_grad = jnp.einsum("rd,ra->da", normed_first, flat_key, preferred_element_type=jnp.float32)
    value_grad = jnp.einsum(
        "rd,ra->da", normed_first, flat_value, preferred_element_type=jnp.float32
    )
    grad_normed_first = (
        jnp.einsum("ra,da->rd", flat_query, query_weight, preferred_element_type=jnp.float32)
        + jnp.einsum("ra,da->rd", flat_key, key_weight, preferred_element_type=jnp.float32)
        + jnp.einsum("ra,da->rd", flat_value, value_weight, preferred_element_type=jnp.float32)
    )
    query_sums = jnp.sum(flat_query.reshape(images, length, -1).astype(jnp.float32), axis=1)
    value_sums = jnp.sum(flat_value.reshape(images, length, -1).astype(jnp.float32), axis=1)
    embedding_wide = embedding.astype(jnp.float32)
    time_query_grad = jnp.dot(embedding_wide.T, query_sums, precision=HIGHEST)
    time_value_grad = jnp.dot(embedding_wide.T, value_sums, precision=HIGHEST)
    contract_last = (((1,), (1,)), ((), ()))
    grad_embed = lax.dot_general(
        query_sums, time_query_weight.astype(jnp.float32), contract_last, precision=HIGHEST
    ) + lax.dot_general(
        value_sums, time_value_weight.astype(jnp.float32), contract_last, precision=HIGHEST
    )
    grad_tok_norm, first_gain_grad, first_shift_grad = norm_backward(
        grad_normed_first, unit_first, inverse_first, first_gain
    )
    tokens_grad = lax.dynamic_slice_in_dim(grad_middle + grad_tok_norm, row_start, own_rows, 0)
    time_table_grad = jnp.dot(onehot.astype(jnp.float32).T, grad_embed, precision=HIGHEST)
    bias_grad = jax.ops.segment_sum(
        score_total.reshape(head_count, -1).T,
        relative_index.reshape(-1),
        num_segments=bias_table.shape[0],
    )

    def own_block(array, axis_number):
        extent = array.shape[axis_number] // model_size
        return lax.dynamic_slice_in_dim(array, model_rank * extent, extent, axis_number)

    query_grad = own_block(query_grad, 1)
    key_grad = own_block(key_grad, 1)
    value_grad = own_block(value_grad, 1)
    time_query_grad = own_block(time_query_grad, 1)
    time_value_grad = own_block(time_value_grad, 1)
    out_grad = own_block(out_grad, 0)
    bias_grad = own_block(bias_grad, 1)
    attention_list = [
        own_block(time_table_grad, 1),
        query_grad,
        key_grad,
        value_grad,
        time_query_grad,
        time_value_grad,
        out_grad,
        own_block(out_bias_grad, 0),
        own_block(first_gain_grad, 0),
        own_block(first_shift_grad, 0),
        own_block(second_gain_grad, 0),
        own_block(second_shift_grad, 0),
        own_block(down_bias_grad, 0),
        bias_grad,
    ]
    merged = reduce_all(attention_list + [up_grad, up_bias_grad, down_grad])
    attention_list = merged[:14]
    up_grad, up_bias_grad, down_grad = (merged[14], merged[15], merged[16])
    return (
        block_out,
        tokens_grad,
        attention_list[0],
        attention_list[1],
        attention_list[2],
        attention_list[3],
        attention_list[4],
        attention_list[5],
        attention_list[6],
        attention_list[7],
        attention_list[8],
        attention_list[9],
        attention_list[10],
        attention_list[11],
        up_grad,
        up_bias_grad,
        down_grad,
        attention_list[12],
        attention_list[13],
    )


def solution(mesh):
    placed = (
        P("dp", None),
        P("dp"),
        P(),
        P(),
        P(),
        P(),
        P(),
        P(),
        P(),
        P(),
        P(),
        P(),
        P(),
        P(),
        P(),
        P(None, "mp"),
        P("mp"),
        P("mp", None),
        P(),
        P(),
        P(("dp", "mp"), None),
    )
    return jax.shard_map(
        on_device,
        mesh=mesh,
        in_specs=placed,
        out_specs=(
            P(("dp", "mp"), None),
            P(("dp", "mp"), None),
            P(None, "mp"),
            P(None, "mp"),
            P(None, "mp"),
            P(None, "mp"),
            P(None, "mp"),
            P(None, "mp"),
            P("mp", None),
            P("mp"),
            P("mp"),
            P("mp"),
            P("mp"),
            P("mp"),
            P(None, "mp"),
            P("mp"),
            P("mp", None),
            P("mp"),
            P(None, "mp"),
        ),
        check_vma=False,
    )
```

profile of v0, /device:TPU:0, one launch (start us, length us, event | category | flops | bytes accessed | tf_op | source)
XLA Modules:
  0.0 2626.3 jit_solution(4509515822518911236)
XLA Ops:
  20.3 7.4 reshape.225
  47.3 7.4 reshape.226
  71.6 9.9 reshape.279
  81.5 7.1 copy.142
  89.8 217.0 %gather_fusion = f32[65536,16]{1,0:T(8,128)} fusion(f32[961,16]{1,0:T(8,128)S(1)} %copy.138, s32[65536]{0:T(1024)S(1)} %broadcast_clamp_fusion), kind=kCustom, calls=%fused_computation | custom fusion | bytes 8650752 | tf_op jit(solution)/shard_map/jit(_take)/gather | solution.py:154
  306.8 20.0 copy.139
  334.9 21.8 while.29
  363.3 7.3 fusion.92
  379.7 8.4 convert_reduce_fusion.3
  396.5 8.9 fusion.78
  412.2 9.2 fusion.77
  428.0 63.6 %all-reduce.7.cloned.1.call-done = f32[1024,1152]{1,0:T(8,128)} async-done(((f32[1024,1152]{1,0:T(8,128)}), f32[1024,1152]{1,0:T(8,128)}) %all-reduce.7.cloned.1.call-update) | async-done | bytes 4718608 | tf_op jit(solution)/shard_map/psum | solution.py:196
  511.8 9.6 reshape.277
  521.3 7.1 copy.147
  531.6 70.8 %while.30 = (s32[]{:T(128)}, f32[16,256,256]{1,2,0:T(8,128)}, bf16[2,2,256,16,72]{2,4,3,1,0:T(8,128)(2,1)}, bf16[2,2,256,16,72]{2,1,0,4,3:T(2,128)(2,1)}, bf16[2...) while((s32[]{:T(128)}, f32[16,256,256]{1,2,0:T(8,128)}, ...), condition=%wide.region_15.16_spmd.clone, body=%wide.region_12.15_spmd.clone.sunk | while | flops 1549590528 | bytes 281777152 | solution.py:223
  541.6 9.4 convert_reduce_fusion.7
  576.2 9.4 convert_reduce_fusion.7
  622.4 8.3 fusion.97
  642.9 8.3 fusion.98
  692.4 16.9 copy.159
  709.2 347.5 %scatter_custom_fusion = f32[961,16]{1,0:T(8,128)S(1)} fusion(s32[65536]{0:T(1024)} %bitcast.175, f32[65536,16]{1,0:T(8,128)} %copy.159, f32[]{:T(128)} %constant.84.clone.1), kind=kCustom, calls=%fused_computation.117 | custom fusion | flops 1048576 | bytes 62016 | tf_op jit(solution)/shard_map/scatter-add | solution.py:259
  1065.6 8.3 fusion.81
  1074.0 8.8 fusion.84
  1130.7 172.7 %concatenate.3 = f32[4939588]{0:T(1024)} concatenate(f32[288000]{0:T(1024)} %reshape.232, f32[331776]{0:T(1024)} %reshape.233, f32[331776]{0:T(1024)} %reshape.234, f32[331776]{0:T(1024)} %reshape.235, f32[331776]{0:T(1024)} %reshape.236, f32[331776]{0:T(1024)} %reshape.237, f32[331776]{0:T(1024)} %reshape.238, f32[288]{0:T(512)S(1)} %dynamic_slice.83, f32[288]{0:T(512)S(1)} %dynamic_slice.84, ...), dimensions={0} | concatenate | bytes 39516704 | tf_op jit(solution)/shard_map/concatenate | solution.py:77
  1303.4 15.7 pad.4
  1319.2 8.8 convolution_convert_fusion.1
  1329.9 582.2 %all-reduce.11.cloned.1.call-done = f32[4939592]{0:T(1024)} async-done(((f32[4939592]{0:T(1024)}), f32[4939592]{0:T(1024)}) %all-reduce.11.cloned.1.call-update) | async-done | bytes 19758384
  1915.9 7.9 broadcast.124
  1923.8 21.8 dynamic-update-slice
  1951.6 592.8 %all-reduce.9.cloned.1.call-done = f32[4939592]{0:T(1024)} async-done(((f32[4939592]{0:T(1024)}), f32[4939592]{0:T(1024)}) %all-reduce.9.cloned.1.call-update) | async-done | bytes 19758384
  2544.5 8.0 fusion.89
  2552.5 6.9 reshape.250
  (311 shorter events, 393.0 us)
Async XLA Ops:
  7.2 7.5 copy-start
  7.2 7.5 copy-start.39
  7.2 7.5 copy-start.53
  7.2 366.2 %all-gather.2.cloned.1.call-start = ((), (), s32[]{:S(2)}) async-start(), calls=%async_computation.2 | async-start | bytes 2949120 | tf_op jit(solution)/shard_map/all_gather | solution.py:181
  8.0 483.6 %all-reduce.7.cloned.1.call-start = ((), (), s32[]{:S(2)}) async-start(), calls=%async_computation.3 | async-start | bytes 9437184 | tf_op jit(solution)/shard_map/psum | solution.py:196
  12.3 53.5 %copy-start.34 = (f32[1024]{0:T(1024)}, f32[1024]{0:T(1024)S(1)}, u32[]{:S(2)}) copy-start(f32[1024]{0:T(1024)S(1)} %broadcast_multiply_fusion.6) | copy-start | bytes 12292
  14.8 51.0 %copy-start.37 = (f32[1024]{0:T(1024)}, f32[1024]{0:T(1024)S(1)}, u32[]{:S(2)}) copy-start(f32[1024]{0:T(1024)S(1)} %add_rsqrt_fusion.1) | copy-start | bytes 12292
  20.3 7.4 copy-start.44
  29.8 24.8 copy-start.32
  33.5 7.4 copy-start.48
  58.3 7.4 copy-start.49
  394.7 1517.4 %all-reduce.11.cloned.1.call-start = ((), (), s32[]{:S(2)}) async-start(), calls=%async_computation.5 | async-start | bytes 39518208
  551.0 11.1 slice-start
  585.5 12.4 slice-start
  602.4 8.5 copy-start.25
  622.4 8.4 copy-start.17
  622.4 8.4 copy-start.30
  622.4 8.4 copy-start.35
  622.4 8.4 copy-start.38
  622.4 8.4 copy-start.40
  622.4 8.4 copy-start.54
  642.9 8.3 copy-start.18
  642.9 8.3 copy-start.31
  651.2 9.5 copy-start.33
  1059.0 14.9 slice-start.2
  1065.6 8.3 copy-start.19
  1065.6 8.3 copy-start.22
  1065.6 8.3 slice-start.3
  1118.7 12.0 copy-start.42
  1319.1 8.9 copy-start.43
  1319.1 630.1 %reduce-scatter.2.cloned.1.call-start = ((), (), s32[]{:S(2)}) async-start(), calls=%async_computation.1 | async-start | bytes 2949120 | tf_op jit(solution)/shard_map/reduce_scatter | solution.py:168
  1328.0 1216.5 %all-reduce.9.cloned.1.call-start = ((), (), s32[]{:S(2)}) async-start(), calls=%async_computation.4 | async-start | bytes 39518208
  (48 other events, 218.2 us)
Sparse Core Ops, SparseCore 0:
  9.6 26.7 all-gather.1
  394.9 96.6 all-reduce.6
  1319.2 592.8 all-reduce.10
  1915.0 32.1 reduce-scatter.1
  1951.8 592.6 all-reduce.8
where the time goes:
time: 2650 us; the launch traced here: 2630 us
  waiting for transfers between devices  1240 us (47%)
  local copies, waits for them, and re-layouts  757 us (29%)
  other arithmetic  425 us (16%)
  matrix products  188 us (7%)
    unnamed x7, waiting for transfers between devices  1180 us
    scatter-add x1, other arithmetic, on_device(): jax.ops.segment_sum(score_total.reshape(head_count, -1).T, relative_index...  347 us
    gather x2, local copies, waits for them, and re-layouts, on_device(): jnp.take(bias_table, relative_index, axis=0)  237 us
    concatenate x1, local copies, waits for them, and re-layouts, padded_vector(): flat_vector = jnp.concatenate([member.reshape(-1) for member in arrays])  173 us
    unnamed x106, local copies, waits for them, and re-layouts  74.1 us
    psum x1, waiting for transfers between devices, on_device(): grad_normed = lax.psum(grad_normed_part, 'mp')  63.6 us
  transfers between devices with their start and end apart: 5, of which 3 were waited for; matrix products, arithmetic and copies ran while one was open for 17% of the time, Pallas kernels for 0%

commit v1 on v0

v1 whole, which is shorter than its diff:
```python
import math
from functools import partial

import jax
import jax.numpy as jnp
from jax import lax
from jax.experimental import pallas as pl
from jax.experimental.pallas import tpu as pltpu
from jax.sharding import PartitionSpec as P

EPSILON = 1e-06
HIGHEST = lax.Precision.HIGHEST
F32 = jnp.float32
BF16 = jnp.bfloat16
LANES = 128
VMEM_BYTES = 60 * 1024 * 1024


def mm(left, right):
    return lax.dot_general(left, right, (((1,), (0,)), ((), ())), preferred_element_type=F32)


def mm_nt(left, right):
    return lax.dot_general(left, right, (((1,), (1,)), ((), ())), preferred_element_type=F32)


def mm_tn(left, right):
    return lax.dot_general(left, right, (((0,), (0,)), ((), ())), preferred_element_type=F32)


def round_up(value, step):
    return -(-value // step) * step


def head_window(slot, head_width):
    first = slot * head_width // LANES * LANES
    last = round_up((slot + 1) * head_width, LANES)
    return first, last - first, slot * head_width - first


def head_mask(lanes, offset, head_width):
    lane = lax.broadcasted_iota(jnp.int32, (1, lanes), 1)
    return jnp.where((lane >= offset) & (lane < offset + head_width), 1.0, 0.0).astype(BF16)


def unit_rows(values):
    centred = values - jnp.mean(values, axis=-1, keepdims=True)
    inverse = lax.rsqrt(jnp.mean(centred * centred, axis=-1, keepdims=True) + EPSILON)
    return centred * inverse, inverse


def norm_back(grad_out, unit, inverse, gain_row):
    grad_unit = grad_out * gain_row
    first_mean = jnp.mean(grad_unit, axis=-1, keepdims=True)
    second_mean = jnp.mean(grad_unit * unit, axis=-1, keepdims=True)
    return inverse * (grad_unit - first_mean - unit * second_mean)


def add_tiles(tiles, product, first):
    for part in range(product.shape[1] // LANES):
        place = first // LANES + part
        piece = product[:, part * LANES : (part + 1) * LANES]
        tiles[place] = piece if tiles[place] is None else tiles[place] + piece


def squeeze_matrix(side):
    wide = lax.broadcasted_iota(jnp.int32, (2 * LANES, LANES), 0)
    close = lax.broadcasted_iota(jnp.int32, (2 * LANES, LANES), 1)
    same = (wide // (2 * side) == close // side) & (wide % (2 * side) == close % side)
    return jnp.where(same, 1.0, 0.0).astype(BF16)


def split_two(values):
    high = values.astype(BF16)
    return high, (values - high.astype(F32)).astype(BF16)


def attend_kernel(
    dims,
    place_ref,
    tokens_ref,
    embed_ref,
    table_ref,
    first_gain,
    first_shift,
    second_gain,
    second_shift,
    out_bias,
    query_hbm,
    key_hbm,
    value_hbm,
    time_query_hbm,
    time_value_hbm,
    out_hbm,
    query_ref,
    key_ref,
    value_ref,
    probs_ref,
    mixed_ref,
    middle_ref,
    normed_ref,
    weights,
    wide_high,
    wide_low,
    windows,
    flat,
    sems,
):
    groups, slots, head_width, side, scale = dims
    group_width = slots * head_width
    sources = (query_hbm, key_hbm, value_hbm, time_query_hbm, time_value_hbm, out_hbm)
    order = (0, 3, 1, 2, 4, 5)
    copies = {}
    for item in order:
        copies[item] = pltpu.make_async_copy(sources[item], weights.at[item], sems.at[item])
        copies[item].start()
    heads = groups * slots
    row_lanes = table_ref.shape[1]
    for head in range(heads):
        row = jnp.broadcast_to(table_ref[head : head + 1, :], (side, row_lanes))
        shifted = pltpu.roll(row, row_lanes - (side - 1), 1, stride=1, stride_axis=0)
        high, low = split_two(shifted)
        wide_high[head * side : (head + 1) * side, :] = high
        wide_low[head * side : (head + 1) * side, :] = low
    squeeze = squeeze_matrix(side)
    for part in range(row_lanes // (2 * LANES)):
        span = slice(part * 2 * LANES, (part + 1) * 2 * LANES)
        narrow = mm(wide_high[:, span], squeeze) + mm(wide_low[:, span], squeeze)
        windows[:, :, part * LANES : (part + 1) * LANES] = narrow.reshape(heads, side, LANES)
    own = mm(place_ref[...], tokens_ref[...])
    unit, _ = unit_rows(own)
    normed = (unit * first_gain[...] + first_shift[...]).astype(BF16)

    def into_groups(rows, target):
        fill = jnp.zeros((rows.shape[0], target.shape[2] - group_width), rows.dtype)
        for group in range(groups):
            piece = rows[:, group * group_width : (group + 1) * group_width]
            target[group] = jnp.concatenate([piece, fill], axis=1)

    copies[0].wait()
    product = mm(normed, weights[0])
    copies[3].wait()
    product = product + mm(embed_ref[...], weights[3])[0:1]
    into_groups(product.astype(BF16), query_ref)
    copies[1].wait()
    into_groups(mm(normed, weights[1]).astype(BF16), key_ref)
    copies[2].wait()
    product = mm(normed, weights[2])
    copies[4].wait()
    product = product + mm(embed_ref[...], weights[4])[0:1]
    into_groups(product.astype(BF16), value_ref)
    length = own.shape[0]
    span_lanes = windows.shape[2]

    def one_group(group, carry):
        tiles = [None] * (query_ref.shape[2] // LANES)
        for slot in range(slots):
            head = group * slots + slot
            first, lanes, offset = head_window(slot, head_width)
            mask = head_mask(lanes, offset, head_width)
            window = windows[head]
            blocks = [None] * side
            steps = LANES // side
            for turn in range(steps):
                turned = window
                if turn:
                    turned = pltpu.roll(window, span_lanes - turn * side, 1)
                for jump in range(-(-side // steps)):
                    block = side - 1 - (jump * steps + turn)
                    if block >= 0:
                        blocks[block] = turned[:, jump * LANES : jump * LANES + length]
            bias = jnp.concatenate(blocks, axis=0)
            keys = key_ref[group, :, first : first + lanes]
            queries = query_ref[group, :, first : first + lanes] * mask
            scores = mm_nt(keys, queries) * scale + bias
            weights_now = jnp.exp(scores - jnp.max(scores, axis=0, keepdims=True))
            totals = jnp.sum(weights_now, axis=0, keepdims=True)
            probs = (weights_now * (1.0 / totals)).astype(BF16)
            probs_ref[head] = probs
            values = value_ref[group, :, first : first + lanes] * mask
            add_tiles(tiles, mm_tn(probs, values), first)
        mixed_ref[group] = jnp.concatenate(tiles, axis=1).astype(BF16)
        return carry

    lax.fori_loop(0, groups, one_group, 0)
    for group in range(groups):
        flat[:, group * group_width : (group + 1) * group_width] = mixed_ref[group][:, :group_width]
    copies[5].wait()
    middle = own + mm(flat[...], weights[5]) + out_bias[...]
    middle_ref[...] = middle
    unit, _ = unit_rows(middle)
    normed_ref[...] = (unit * second_gain[...] + second_shift[...]).astype(BF16)


def normed_kernel(rank_ref, place_ref, tokens_ref, gain, shift, normed_ref):
    unit, _ = unit_rows(mm(place_ref[...], tokens_ref[...]))
    normed_ref[...] = (unit * gain[...] + shift[...]).astype(BF16)


def gelu_pair(hidden):
    root = math.sqrt(2.0 / math.pi)
    square = hidden * hidden
    bend = jnp.tanh(hidden * (root + (root * 0.044715) * square))
    half = 0.5 + 0.5 * bend
    slope = half + (0.5 * hidden) * (1.0 - bend * bend) * (root + (3.0 * root * 0.044715) * square)
    return hidden * half, slope


def feed_kernel(chunks, *refs):
    normed = refs[:chunks]
    cotangent = refs[chunks : 2 * chunks]
    up_ref, up_bias, down_ref = refs[2 * chunks : 2 * chunks + 3]
    outs = refs[2 * chunks + 3 :]
    out_parts = outs[:chunks]
    grad_parts = outs[chunks : 2 * chunks]
    down_grad, up_grad, up_bias_grad = outs[2 * chunks : 2 * chunks + 3]
    active, grad_hidden, all_normed, all_cotangent = outs[2 * chunks + 3 :]
    rows = normed[0].shape[0]
    bias_total = None
    for chunk in range(chunks):
        span = slice(chunk * rows, (chunk + 1) * rows)
        all_normed[span, :] = normed[chunk][...]
        all_cotangent[span, :] = cotangent[chunk][...]
        hidden = mm(normed[chunk][...], up_ref[...]) + up_bias[...]
        gelu_out, slope = gelu_pair(hidden)
        active[span, :] = gelu_out.astype(BF16)
        back = mm_nt(cotangent[chunk][...], down_ref[...]) * slope
        rounded = back.astype(BF16)
        grad_hidden[span, :] = rounded
        total = jnp.sum(rounded.astype(F32), axis=0, keepdims=True)
        bias_total = total if bias_total is None else bias_total + total
    up_bias_grad[...] = jnp.broadcast_to(bias_total, up_bias_grad.shape)
    down_grad[...] = mm_tn(active[...], all_cotangent[...]).astype(BF16)
    up_grad[...] = mm_tn(all_normed[...], grad_hidden[...]).astype(BF16)
    for chunk in range(chunks):
        span = slice(chunk * rows, (chunk + 1) * rows)
        grad_parts[chunk][...] = mm_nt(grad_hidden[span, :], up_ref[...]).astype(BF16)
    for chunk in range(chunks):
        span = slice(chunk * rows, (chunk + 1) * rows)
        out_parts[chunk][...] = mm(active[span, :], down_ref[...]).astype(BF16)


def middle_kernel(
    own_ref, far_ref, middle_ref, cotangent_ref, gain, grad_ref, branch_ref, sums_ref
):
    grad_normed = own_ref[...].astype(F32) + far_ref[...].astype(F32)
    unit, inverse = unit_rows(middle_ref[...])
    cotangent = cotangent_ref[...].astype(F32)
    grad_middle = cotangent + norm_back(grad_normed, unit, inverse, gain[...])
    grad_ref[...] = grad_middle
    branch_ref[...] = grad_middle.astype(BF16)
    sums_ref[...] = jnp.zeros_like(sums_ref)
    sums_ref[0:1, :] = jnp.sum(grad_normed * unit, axis=0, keepdims=True)
    sums_ref[1:2, :] = jnp.sum(grad_normed, axis=0, keepdims=True)
    sums_ref[2:3, :] = jnp.sum(grad_middle, axis=0, keepdims=True)
    sums_ref[3:4, :] = jnp.sum(cotangent, axis=0, keepdims=True)


def attend_back_kernel(
    dims,
    rank_ref,
    branch_ref,
    query_ref,
    key_ref,
    value_ref,
    probs_ref,
    out_ref,
    packed_ref,
    flat_ref,
    sums_ref,
    table_ref,
    grad_mixed,
    sheared,
    grads,
):
    groups, slots, head_width, side, scale = dims
    group_width = slots * head_width
    rank = rank_ref[0]
    length = branch_ref.shape[0]
    fill = jnp.zeros((length, grad_mixed.shape[2] - group_width), BF16)
    product = mm_nt(branch_ref[...], out_ref[...]).astype(BF16)
    for group in range(groups):
        piece = product[:, group * group_width : (group + 1) * group_width]
        grad_mixed[group] = jnp.concatenate([piece, fill], axis=1)
    span_lanes = sheared.shape[2]

    def one_group(group, carry):
        wide = grad_mixed.shape[2] // LANES
        query_tiles, key_tiles, value_tiles = [None] * wide, [None] * wide, [None] * wide
        for slot in range(slots):
            head = group * slots + slot
            first, lanes, offset = head_window(slot, head_width)
            mask = head_mask(lanes, offset, head_width)
            span = slice(first, first + lanes)
            mixed_now = grad_mixed[group, :, span] * mask
            probs = probs_ref[head]
            grad_probs = mm_nt(value_ref[group, :, span], mixed_now)
            probs_wide = probs.astype(F32)
            weighted = probs_wide * grad_probs
            grad_scores = weighted - probs_wide * jnp.sum(weighted, axis=0, keepdims=True)
            rounded = grad_scores.astype(BF16)
            add_tiles(value_tiles, mm(probs, mixed_now), first)
            add_tiles(key_tiles, mm(rounded, query_ref[group, :, span] * mask), first)
            add_tiles(query_tiles, mm_tn(rounded, key_ref[group, :, span] * mask), first)
            steps = LANES // side
            shear = jnp.zeros((side, span_lanes), F32)
            for turn in range(steps):
                summed = None
                for jump in range(-(-side // steps)):
                    block = side - 1 - (jump * steps + turn)
                    if block >= 0:
                        piece = grad_scores[block * side : (block + 1) * side, :]
                        parts = []
                        if jump:
                            parts.append(jnp.zeros((side, jump * LANES), F32))
                        parts.append(piece)
                        rest = span_lanes - jump * LANES - length
                        if rest:
                            parts.append(jnp.zeros((side, rest), F32))
                        piece = jnp.concatenate(parts, axis=1)
                        summed = piece if summed is None else summed + piece
                shear = shear + (pltpu.roll(summed, turn * side, 1) if turn else summed)
            sheared[:, pl.ds(head, 1), :] = shear[:, None, :]
        grads[0, group] = (jnp.concatenate(query_tiles, axis=1) * scale).astype(BF16)
        grads[1, group] = (jnp.concatenate(key_tiles, axis=1) * scale).astype(BF16)
        grads[2, group] = jnp.concatenate(value_tiles, axis=1).astype(BF16)
        return carry

    lax.fori_loop(0, groups, one_group, 0)
    packed_lanes = packed_ref.shape[2]
    for group in range(groups):
        pieces = [grads[item, group][:, :group_width] for item in range(3)]
        for item in range(3):
            flat_ref[item, :, group * group_width : (group + 1) * group_width] = pieces[item]
        if packed_lanes > 3 * group_width:
            pieces.append(jnp.zeros((length, packed_lanes - 3 * group_width), BF16))
        packed_ref[group ^ rank] = jnp.concatenate(pieces, axis=1)
    sums_ref[...] = jnp.zeros_like(sums_ref)
    sums_ref[0:1, :] = jnp.sum(flat_ref[0].astype(F32), axis=0, keepdims=True)
    sums_ref[1:2, :] = jnp.sum(flat_ref[2].astype(F32), axis=0, keepdims=True)
    squeeze = squeeze_matrix(side)
    heads = groups * slots
    table = jnp.zeros(table_ref.shape, F32)
    for column in range(side):
        high, low = split_two(sheared[column])
        parts = []
        for part in range(span_lanes // LANES):
            span = slice(part * LANES, (part + 1) * LANES)
            parts.append(mm_nt(high[:, span], squeeze) + mm_nt(low[:, span], squeeze))
        spread = jnp.concatenate(parts, axis=1)
        turn = side - 1 - column
        table = table + (pltpu.roll(spread, turn, 1) if turn else spread)
    table_ref[...] = table


def tokens_kernel(
    flat_ref,
    query_ref,
    key_ref,
    value_ref,
    tokens_ref,
    place_ref,
    gain,
    middle_ref,
    grad_ref,
    sums_ref,
):
    grad_normed = (
        mm_nt(flat_ref[0], query_ref[...])
        + mm_nt(flat_ref[1], key_ref[...])
        + mm_nt(flat_ref[2], value_ref[...])
    )
    unit, inverse = unit_rows(mm(place_ref[...], tokens_ref[...]))
    total = middle_ref[...] + norm_back(grad_normed, unit, inverse, gain[...])
    high, low = split_two(total)
    grad_ref[...] = mm_tn(place_ref[...], high) + mm_tn(place_ref[...], low)
    sums_ref[...] = jnp.zeros_like(sums_ref)
    sums_ref[0:1, :] = jnp.sum(grad_normed * unit, axis=0, keepdims=True)
    sums_ref[1:2, :] = jnp.sum(grad_normed, axis=0, keepdims=True)


def weights_kernel(chunks, group_width, *refs):
    normed = refs[0]
    packed = refs[1 : 1 + chunks]
    branch = refs[1 + chunks : 1 + 2 * chunks]
    mixed = refs[1 + 2 * chunks : 1 + 3 * chunks]
    out_ref, all_packed, all_branch, all_mixed = refs[1 + 3 * chunks :]
    rows = packed[0].shape[0]
    for chunk in range(chunks):
        span = slice(chunk * rows, (chunk + 1) * rows)
        all_packed[span, :] = packed[chunk][...]
        all_branch[span, :] = branch[chunk][...]
        all_mixed[span, :] = mixed[chunk][...]
    left = mm_tn(normed[...], all_packed[...]).astype(BF16)
    right = mm_tn(all_branch[...], all_mixed[...]).astype(BF16)
    out_ref[...] = jnp.concatenate([left[:, : 3 * group_width], right[:, :group_width]], axis=1)


def call(kernel, outs, scratch=(), flops=0, moved=0, **extra):
    return pl.pallas_call(
        kernel,
        out_shape=outs,
        scratch_shapes=list(scratch),
        compiler_params=pltpu.CompilerParams(vmem_limit_bytes=VMEM_BYTES),
        cost_estimate=pl.CostEstimate(flops=flops, bytes_accessed=moved, transcendentals=0),
        **extra,
    )


def shape_of(*sizes, dtype=BF16):
    return jax.ShapeDtypeStruct(sizes, dtype)


VMEM = pl.BlockSpec(memory_space=pltpu.VMEM)
HBM = pl.BlockSpec(memory_space=pl.ANY)
SMEM = pl.BlockSpec(memory_space=pltpu.SMEM)


def swap(array, axis, distance):
    size = lax.axis_size(axis)
    return lax.ppermute(array, axis, [(i, i ^ distance) for i in range(size)])


def add_low(left, right):
    return (left.astype(F32) + right.astype(F32)).astype(BF16)


def reduce_over_dp(unit, order):
    rank = lax.axis_index("dp")
    halves = order[:2]
    current = unit
    for level in halves:
        bit = (rank >> level) & 1
        half = current.shape[0] // 2
        sent = lax.dynamic_slice_in_dim(current, (1 - bit) * half, half, 0)
        kept = lax.dynamic_slice_in_dim(current, bit * half, half, 0)
        current = add_low(kept, swap(sent, "dp", 1 << level))
    for level in order[2:]:
        current = add_low(current, swap(current, "dp", 1 << level))
    for level in halves[::-1]:
        bit = (rank >> level) & 1
        other = swap(current, "dp", 1 << level)
        current = jnp.where(
            bit == 0,
            jnp.concatenate([current, other], axis=0),
            jnp.concatenate([other, current], axis=0),
        )
    return current


def on_device(
    tokens,
    timesteps,
    relative_index,
    time_table,
    query_weight,
    key_weight,
    value_weight,
    time_query_weight,
    time_value_weight,
    out_weight,
    out_bias,
    first_gain,
    first_shift,
    second_gain,
    second_shift,
    up_weight,
    up_bias,
    down_weight,
    down_bias,
    bias_table,
    cotangent,
):
    length = relative_index.shape[0]
    width = tokens.shape[1]
    heads = bias_table.shape[1]
    head_width = width // heads
    side = math.isqrt(length)
    groups = lax.axis_size("mp")
    dp_size = lax.axis_size("dp")
    rank = lax.axis_index("mp")
    slots = heads // groups
    group_width = slots * head_width
    group_lanes = round_up(group_width, LANES)
    packed_lanes = round_up(3 * group_width, LANES)
    hidden_width = up_weight.shape[1]
    dims = (groups, slots, head_width, side, head_width ** (-0.5))
    ranks = jnp.reshape(rank, (1,)).astype(jnp.int32)
    row = lambda vector: vector.reshape(1, -1)

    stride = 2 * side - 1
    first_row = relative_index[0]
    row_part = first_row // stride
    column_part = first_row % stride
    cells = (jnp.max(row_part) - row_part) * side + jnp.max(column_part) - column_part
    place = (jnp.arange(length, dtype=jnp.int32)[:, None] == cells[None, :]).astype(BF16)
    own_cotangent = mm(place, cotangent).astype(BF16)

    def gather_mp(own):
        near = swap(own, "mp", 1)
        far = swap(own, "mp", 2)
        return [own, near, far, swap(far, "mp", 1)]

    all_cotangent = gather_mp(own_cotangent)
    own_tokens = lax.dynamic_slice_in_dim(tokens, rank * length, length, 0)
    own_step = lax.dynamic_index_in_dim(timesteps, rank, 0, keepdims=False)
    own_embed = lax.dynamic_slice_in_dim(time_table, own_step, 1, 0)
    embed_rows = jnp.broadcast_to(own_embed, (16, width))
    table_lanes = 2 * side
    table = jnp.pad(
        bias_table.T.reshape(heads, stride, stride), ((0, 0), (0, 1), (0, 1))
    ).reshape(heads, table_lanes * table_lanes)
    span_lanes = table_lanes * side
    outs = call(
        partial(attend_kernel, dims),
        [
            shape_of(groups, length, group_lanes),
            shape_of(groups, length, group_lanes),
            shape_of(groups, length, group_lanes),
            shape_of(heads, length, length),
            shape_of(groups, length, group_lanes),
            shape_of(length, width, dtype=F32),
            shape_of(length, width),
        ],
        [
            pltpu.VMEM((6, width, width), BF16),
            pltpu.VMEM((heads * side, table_lanes * table_lanes), BF16),
            pltpu.VMEM((heads * side, table_lanes * table_lanes), BF16),
            pltpu.VMEM((heads, side, span_lanes), F32),
            pltpu.VMEM((length, width), BF16),
            pltpu.SemaphoreType.DMA((6,)),
        ],
        flops=8 * length * width * width,
        moved=24 * width * width,
        in_specs=[VMEM] * 9 + [HBM] * 6,
    )(
        place,
        own_tokens,
        embed_rows,
        table,
        row(first_gain),
        row(first_shift),
        row(second_gain),
        row(second_shift),
        row(out_bias),
        query_weight,
        key_weight,
        value_weight,
        time_query_weight,
        time_value_weight,
        out_weight,
    )
    query_rows, key_rows, value_rows, probs, mixed, middle, normed_second = outs
    all_normed = gather_mp(normed_second)

    normed_first = pl.pallas_call(
        normed_kernel,
        out_shape=shape_of(groups * length, width),
        grid_spec=pltpu.PrefetchScalarGridSpec(
            num_scalar_prefetch=1,
            grid=(groups,),
            in_specs=[
                pl.BlockSpec((length, length), lambda i, me: (0, 0)),
                pl.BlockSpec((length, width), lambda i, me: (i ^ me[0], 0)),
                pl.BlockSpec((1, width), lambda i, me: (0, 0)),
                pl.BlockSpec((1, width), lambda i, me: (0, 0)),
            ],
            out_specs=pl.BlockSpec((length, width), lambda i, me: (i, 0)),
        ),
    )(ranks, place, tokens, row(first_gain), row(first_shift))

    rows = groups * length
    feed = call(
        partial(feed_kernel, groups),
        [shape_of(length, width)] * (2 * groups)
        + [
            shape_of(hidden_width, width),
            shape_of(width, hidden_width),
            shape_of(8, hidden_width, dtype=F32),
        ],
        [
            pltpu.VMEM((rows, hidden_width), BF16),
            pltpu.VMEM((rows, hidden_width), BF16),
            pltpu.VMEM((rows, width), BF16),
            pltpu.VMEM((rows, width), BF16),
        ],
        flops=12 * rows * width * hidden_width,
        moved=8 * width * hidden_width,
    )(*all_normed, *all_cotangent, up_weight, row(up_bias), down_weight)
    out_parts = feed[:groups]
    grad_parts = feed[groups : 2 * groups]
    down_grad, up_grad, up_bias_sum = feed[2 * groups :]

    levels = list(range(dp_size.bit_length() - 1))
    other_order = levels[1:2] + levels[:1] + levels[2:]

    def scatter_mp(parts):
        kept = parts[0].astype(F32) + swap(parts[1], "mp", 1).astype(F32)
        sent = add_low(parts[2], swap(parts[3], "mp", 1))
        return kept, swap(sent, "mp", 2)

    grad_own, grad_far = scatter_mp(grad_parts)
    down_total = reduce_over_dp(down_grad, levels)
    up_total = reduce_over_dp(up_grad, other_order)

    grad_middle, grad_branch, middle_sums = call(
        middle_kernel,
        [
            shape_of(length, width, dtype=F32),
            shape_of(length, width),
            shape_of(8, width, dtype=F32),
        ],
    )(grad_own, grad_far, middle, own_cotangent, row(second_gain))
    all_branch = gather_mp(grad_branch)

    packed, flat_grads, head_sums, table_grad = call(
        partial(attend_back_kernel, dims),
        [
            shape_of(groups, length, packed_lanes),
            shape_of(3, length, width),
            shape_of(8, width, dtype=F32),
            shape_of(heads, table_lanes * table_lanes, dtype=F32),
        ],
        [
            pltpu.VMEM((groups, length, group_lanes), BF16),
            pltpu.VMEM((side, heads, span_lanes), F32),
            pltpu.VMEM((3, groups, length, group_lanes), BF16),
        ],
        flops=2 * length * width * width,
        moved=4 * width * width,
        in_specs=[SMEM] + [VMEM] * 6,
    )(ranks, grad_branch, query_rows, key_rows, value_rows, probs, out_weight)

    def exchange_mp(parts):
        return [parts[0]] + [swap(parts[j], "mp", j) for j in range(1, groups)]

    all_packed = exchange_mp([packed[j] for j in range(groups)])
    mixed_turned = [
        lax.dynamic_index_in_dim(mixed, rank ^ j, 0, keepdims=False) for j in range(groups)
    ]
    all_mixed = exchange_mp(mixed_turned)

    tokens_grad, token_sums = call(
        tokens_kernel,
        [shape_of(length, width, dtype=F32), shape_of(8, width, dtype=F32)],
        flops=6 * length * width * width,
        moved=6 * width * width,
    )(
        flat_grads,
        query_weight,
        key_weight,
        value_weight,
        own_tokens,
        place,
        row(first_gain),
        grad_middle,
    )

    unit = call(
        partial(weights_kernel, groups, group_width),
        shape_of(width, 4 * group_width),
        [
            pltpu.VMEM((rows, packed_lanes), BF16),
            pltpu.VMEM((rows, width), BF16),
            pltpu.VMEM((rows, group_lanes), BF16),
        ],
        flops=8 * rows * width * group_width,
        moved=8 * rows * width,
    )(normed_first, *all_packed, *all_branch, *all_mixed)
    unit_total = reduce_over_dp(unit, levels).astype(F32)
    query_grad, key_grad, value_grad, out_grad = [
        unit_total[:, j * group_width : (j + 1) * group_width] for j in range(4)
    ]
    out_grad = out_grad.T

    step_row = jnp.full((1, width), own_step, F32)
    image_rows = jnp.concatenate(
        [head_sums[0:2], own_embed.astype(F32), step_row, jnp.zeros((4, width), F32)], axis=0
    )
    image_all = lax.all_gather(image_rows, ("dp", "mp"), axis=0, tiled=True)
    image_all = image_all.reshape(-1, 8, width)
    query_sums, value_sums, embed_all = image_all[:, 0], image_all[:, 1], image_all[:, 2]
    steps_all = image_all[:, 3, 0].astype(jnp.int32)

    def own_block(array, axis_number):
        extent = array.shape[axis_number] // groups
        return lax.dynamic_slice_in_dim(array, rank * extent, extent, axis_number)

    contract_first = (((0,), (0,)), ((), ()))
    contract_last = (((1,), (1,)), ((), ()))
    time_query_grad = lax.dot_general(
        embed_all, own_block(query_sums, 1), contract_first, precision=HIGHEST
    )
    time_value_grad = lax.dot_general(
        embed_all, own_block(value_sums, 1), contract_first, precision=HIGHEST
    )
    grad_embed = lax.dot_general(
        query_sums, own_block(time_query_weight, 0).astype(F32), contract_last, precision=HIGHEST
    ) + lax.dot_general(
        value_sums, own_block(time_value_weight, 0).astype(F32), contract_last, precision=HIGHEST
    )
    onehot = jnp.arange(time_table.shape[0], dtype=jnp.int32)[:, None] == steps_all[None, :]
    time_table_grad = jnp.dot(onehot.astype(F32), grad_embed, precision=HIGHEST)

    vectors = jnp.concatenate([middle_sums[0:4], token_sums[0:2]], axis=0)
    vectors = vectors.reshape(6, groups, group_width).transpose(1, 0, 2).reshape(groups, -1)
    short = jnp.concatenate([vectors, table_grad.reshape(groups, -1)], axis=1)
    for level in range(groups.bit_length() - 1):
        short = short + swap(short, "mp", 1 << level)
    short = lax.dynamic_index_in_dim(short, rank, 0, keepdims=False)
    short = jnp.concatenate([short, up_bias_sum[0]])
    for level in levels:
        short = short + swap(short, "dp", 1 << level)
    parts = [short[j * group_width : (j + 1) * group_width] for j in range(6)]
    second_gain_grad, second_shift_grad, out_bias_grad, down_bias_grad = parts[:4]
    first_gain_grad, first_shift_grad = parts[4:]
    table_size = slots * table_lanes * table_lanes
    table_own = short[6 * group_width : 6 * group_width + table_size]
    table_own = table_own.reshape(slots, table_lanes, table_lanes)[:, :stride, :stride]
    bias_table_grad = table_own.reshape(slots, stride * stride).T
    up_bias_grad = short[6 * group_width + table_size :]

    out_own, out_far = scatter_mp(out_parts)
    block_out = (middle + out_own + out_far.astype(F32) + down_bias).astype(BF16)
    block_out = mm_tn(place, block_out).astype(BF16)
    return (
        block_out,
        tokens_grad,
        time_table_grad,
        query_grad,
        key_grad,
        value_grad,
        time_query_grad,
        time_value_grad,
        out_grad,
        out_bias_grad,
        first_gain_grad,
        first_shift_grad,
        second_gain_grad,
        second_shift_grad,
        up_total.astype(F32),
        up_bias_grad,
        down_total.astype(F32),
        down_bias_grad,
        bias_table_grad,
    )


def solution(mesh):
    whole = P()
    rows = P(("dp", "mp"), None)
    columns = P(None, "mp")
    split = P("mp")
    placed = (
        (P("dp", None), P("dp"))
        + (whole,) * 13
        + (columns, split, P("mp", None), whole, whole, rows)
    )
    return jax.shard_map(
        on_device,
        mesh=mesh,
        in_specs=placed,
        out_specs=(rows, rows)
        + (columns,) * 6
        + (P("mp", None),)
        + (split,) * 5
        + (columns, split, P("mp", None), split, columns),
        check_vma=False,
    )
```

time: 2650 us -> 465 us (0.18)
  waiting for transfers between devices: 1240 us -> 218 us
  local copies, waits for them, and re-layouts: 757 us -> 49.3 us
  other arithmetic: 425 us -> 36.5 us
  matrix products: 188 us -> 12.6 us
  Pallas kernels: 0 us -> 83.5 us
  starting transfers between devices: 0.2 us -> 38.5 us
    unnamed x7 -> x1, waiting for transfers between devices: 1180 us -> 0.02 us
    scatter-add x1 -> x0, other arithmetic: 347 us -> none  [on_device(): jax.ops.segment_sum(score_total.reshape(head_count, -1).T, relative_index...]
    gather x2 -> x0, local copies, waits for them, and re-layouts: 237 us -> none  [on_device(): jnp.take(bias_table, relative_index, axis=0)]
    ppermute x0 -> x41, waiting for transfers between devices: none -> 218 us  [swap(): return lax.ppermute(array, axis, [(i, i ^ distance) for i in range(size)])]
    dot_general x40 -> x7, matrix products: 188 us -> 12.6 us  [the longest x1 2.44 us: mm_tn(): lax.dot_general(left, right, (((0,), (0,)), ((), ())), preferred_element_...]
    concatenate x1 -> x2, local copies, waits for them, and re-layouts: 173 us -> 1.17 us  [on_device(): jnp.concatenate([head_sums[0:2], own_embed.astype(F32), step_row, jnp.zer...]
    reshape x27 -> x14, local copies, waits for them, and re-layouts: 123 us -> 10.9 us  [the longest x3 3.75 us: on_device(): vectors.reshape(6, groups, group_width).transpose(1, 0, 2)]
    pallas_call x0 -> x7, Pallas kernels: none -> 83.5 us  [the longest x1 25.6 us: on_device(): call(partial(feed_kernel, groups), [shape_of(length, width)] * (2 * group...]
  transfers between devices with their start and end apart: 5 -> 42, of which waited for: 3 -> 17; matrix products, arithmetic and copies ran while one was open for 17% -> 14% of each run, Pallas kernels for 0% -> 15%
where the time goes in v1:
time: 465 us; the launch traced here: 457 us
  waiting for transfers between devices  218 us (47%)
  Pallas kernels  83.5 us (18%)
  local copies, waits for them, and re-layouts  49.3 us (11%)
  starting transfers between devices  38.5 us (8%)
  other arithmetic  36.5 us (8%)
  between operations  17.7 us (4%)
  matrix products  12.6 us (3%)
    ppermute x41, waiting for transfers between devices, swap(): return lax.ppermute(array, axis, [(i, i ^ distance) for i in range(size)])  218 us
    ppermute x41, starting transfers between devices, swap(): return lax.ppermute(array, axis, [(i, i ^ distance) for i in range(size)])  38.5 us
    pallas_call x1, Pallas kernels, on_device(): call(partial(feed_kernel, groups), [shape_of(length, width)] * (2 * group...  25.6 us
    pallas_call x1, Pallas kernels, on_device(): call(partial(attend_kernel, dims), [shape_of(groups, length, group_lanes)...  15.3 us
    unnamed x78, local copies, waits for them, and re-layouts  14.9 us
    pallas_call x1, Pallas kernels, on_device(): call(partial(attend_back_kernel, dims), [shape_of(groups, length, packed_...  14.4 us
    convert_element_type x11, other arithmetic, add_low(): return (left.astype(F32) + right.astype(F32)).astype(BF16)  9.8 us
    pallas_call x1, Pallas kernels, on_device(): call(tokens_kernel, [shape_of(length, width, dtype=F32), shape_of(8, widt...  9.47 us
  transfers between devices with their start and end apart: 42, of which 17 were waited for; matrix products, arithmetic and copies ran while one was open for 14% of the time, Pallas kernels for 15%

profile of v1, /device:TPU:0, one launch (start us, length us, event | category | flops | bytes accessed | tf_op | source)
XLA Modules:
  0.0 456.5 jit_solution(349270150362799063)
XLA Ops:
  24.1 15.3 %shard_map.348 = (bf16[4,256,384]{2,1,0:T(8,128)(2,1)}, bf16[4,256,384]{2,1,0:T(8,128)(2,1)}, bf16[4,256,384]{2,1,0:T(8,128)(2,1)}, bf16[16,256,256]{2,1,0:T(8,1...) custom-call(bf16[256,256]{1,0:T(8,128)(2,1)} %fusion.8.place_ref, ...), custom_call_target="tpu_custom_call" | custom-call | flops 2717908992 | bytes 31850496 | tf_op jit(solution)/shard_map/pallas_call | solution.py:514
  39.4 3.0 collective-permute-start.1
  43.5 13.3 %collective-permute-done.1.refs_2_ = bf16[256,1152]{1,0:T(8,128)(2,1)S(1)} collective-permute-done((bf16[256,1152]{1,0:T(8,128)(2,1)}, bf16[256,1152]{1,0:T(8,128)(2,1)S(1)}, u32[]{:S(2)}, u32[]{:S(2)}) %collective-permute-start.1) | collective-permute-done | bytes 589856 | tf_op jit(solution)/shard_map/ppermute | solution.py:421
  56.8 11.8 %collective-permute-done.4.refs_6_ = bf16[256,1152]{1,0:T(8,128)(2,1)S(1)} collective-permute-done((bf16[256,1152]{1,0:T(8,128)(2,1)S(1)}, bf16[256,1152]{1,0:T(8,128)(2,1)S(1)}, u32[]{:S(2)}, u32[]{:S(2)}) %collective-permute-start.4) | collective-permute-done | bytes 589856 | tf_op jit(solution)/shard_map/ppermute | solution.py:421
  72.5 5.7 %shard_map.353.refs_0_ = bf16[1024,1152]{1,0:T(8,128)(2,1)} custom-call(s32[1]{0:T(128)} %bitcast.5.rank_ref, bf16[256,256]{1,0:T(8,128)(2,1)} %fusion.8.place_ref, bf16[1024,1152]{1,0:T(8,128)(2,1)} %tokens_ref.1, f32[1,1152]{1,0:T(1,128)} %reshape.105.first_gain.gain, f32[1,1152]{1,0:T(1,128)} %reshape.106.first_shift.shift), custom_call_target="tpu_custom_call" | custom-call | tf_op jit(solution)/shard_map/pallas_call | solution.py:556
  80.0 25.6 %shard_map.349 = (bf16[256,1152]{1,0:T(8,128)(2,1)}, bf16[256,1152]{1,0:T(8,128)(2,1)}, bf16[256,1152]{1,0:T(8,128)(2,1)}, bf16[256,1152]{1,0:T(8,128)(2,1)}, bf...) custom-call(bf16[256,1152]{1,0:T(8,128)(2,1)} %get-tuple-element.47., ...), custom_call_target="tpu_custom_call" | custom-call | flops 16307453952 | bytes 10616832 | tf_op jit(solution)/shard_map/pallas_call | solution.py:573
  106.3 2.6 constant_dynamic-slice_fusion.3
  116.4 11.8 %collective-permute-done.11.far_ref = bf16[256,1152]{1,0:T(8,128)(2,1)S(1)} collective-permute-done((bf16[256,1152]{1,0:T(8,128)(2,1)S(1)}, bf16[256,1152]{1,0:T(8,128)(2,1)S(1)}, u32[]{:S(2)}, u32[]{:S(2)}) %collective-permute-start.11) | collective-permute-done | bytes 589856 | tf_op jit(solution)/shard_map/ppermute | solution.py:421
  129.0 4.2 shard_map.350
  133.2 14.4 %shard_map.351 = (bf16[4,256,896]{2,1,0:T(8,128)(2,1)}, bf16[3,256,1152]{2,1,0:T(8,128)(2,1)}, f32[8,1152]{1,0:T(8,128)}, f32[16,1024]{1,0:T(8,128)}) custom-call(s32[1]{0:T(128)} %bitcast.5.rank_ref, bf16[256,1152]{1,0:T(8,128)(2,1)} %get-tuple-element.56.branch_ref.refs_5_, bf16[4,256,384]{2,1,0:T(8,128)(2,1)} %get-tuple-element.57.query_ref, ...), custom_call_target="tpu_custom_call" | custom-call | flops 679477248 | bytes 5308416 | tf_op jit(solution)/shard_map/pallas_call | solution.py:616
  149.3 9.5 %shard_map.352 = (f32[256,1152]{1,0:T(8,128)}, f32[8,1152]{1,0:T(8,128)}) custom-call(bf16[3,256,1152]{2,1,0:T(8,128)(2,1)} %get-tuple-element.61.flat_ref, bf16[1152,1152]{1,0:T(8,128)(2,1)} %query_ref.1, bf16[1152,1152]{1,0:T(8,128)(2,1)} %key_ref.1, bf16[1152,1152]{1,0:T(8,128)(2,1)} %value_ref.1, ...), custom_call_target="tpu_custom_call" | custom-call | flops 2038431744 | bytes 7962624 | tf_op jit(solution)/shard_map/pallas_call | solution.py:643
  171.6 12.9 %collective-permute-done.27 = f32[4,5824]{1,0:T(4,128)S(1)} collective-permute-done((f32[4,5824]{1,0:T(4,128)S(1)}, f32[4,5824]{1,0:T(4,128)S(1)}, u32[]{:S(2)}, u32[]{:S(2)}) %collective-permute-start.27) | collective-permute-done | bytes 93216 | tf_op jit(solution)/shard_map/ppermute | solution.py:421
  188.4 13.5 %collective-permute-done.28 = f32[6976]{0:T(1024)S(1)} collective-permute-done((f32[6976]{0:T(1024)S(1)}, f32[6976]{0:T(1024)S(1)}, u32[]{:S(2)}, u32[]{:S(2)}) %collective-permute-start.28) | collective-permute-done | bytes 27936 | tf_op jit(solution)/shard_map/ppermute | solution.py:421
  202.6 3.3 collective-permute-done.29
  207.4 2.8 collective-permute-done.20.refs_12_
  213.6 9.6 %collective-permute-done.13.refs_3_ = bf16[256,896]{1,0:T(8,128)(2,1)S(1)} collective-permute-done((bf16[256,896]{1,0:T(8,128)(2,1)S(1)}, bf16[256,896]{1,0:T(8,128)(2,1)S(1)}, u32[]{:S(2)}, u32[]{:S(2)}) %collective-permute-start.13) | collective-permute-done | bytes 458784 | tf_op jit(solution)/shard_map/ppermute | solution.py:421
  225.2 22.0 %collective-permute-done.14.refs_4_ = bf16[256,896]{1,0:T(8,128)(2,1)S(1)} collective-permute-done((bf16[256,896]{1,0:T(8,128)(2,1)S(1)}, bf16[256,896]{1,0:T(8,128)(2,1)S(1)}, u32[]{:S(2)}, u32[]{:S(2)}) %collective-permute-start.14) | collective-permute-done | bytes 458784 | tf_op jit(solution)/shard_map/ppermute | solution.py:421
  253.5 8.9 %shard_map.354 = bf16[1152,1152]{1,0:T(8,128)(2,1)} custom-call(bf16[1024,1152]{1,0:T(8,128)(2,1)} %shard_map.353.refs_0_, bf16[256,896]{1,0:T(8,128)(2,1)} %get-tuple-element.141.refs_1_, bf16[256,896]{1,0:T(8,128)(2,1)} %copy-done.33, bf16[256,896]{1,0:T(8,128)(2,1)} %copy-done.34, bf16[256,896]{1,0:T(8,128)(2,1)} %copy-done.35, ...), custom_call_target="tpu_custom_call" | custom-call | flops 2717908992 | bytes 9437184 | tf_op jit(solution)/shard_map/pallas_call | solution.py:659
  268.1 28.8 %collective-permute-done.33 = bf16[288,1152]{1,0:T(8,128)(2,1)S(1)} collective-permute-done((bf16[288,1152]{1,0:T(8,128)(2,1)S(1)}, bf16[288,1152]{1,0:T(8,128)(2,1)S(1)}, u32[]{:S(2)}, u32[]{:S(2)}) %collective-permute-start.33) | collective-permute-done | bytes 663584 | tf_op jit(solution)/shard_map/ppermute | solution.py:421
  298.6 12.2 %collective-permute-done.38 = bf16[288,1152]{1,0:T(8,128)(2,1)} collective-permute-done((bf16[288,1152]{1,0:T(8,128)(2,1)S(1)}, bf16[288,1152]{1,0:T(8,128)(2,1)}, u32[]{:S(2)}, u32[]{:S(2)}) %collective-permute-start.38) | collective-permute-done | bytes 663584 | tf_op jit(solution)/shard_map/ppermute | solution.py:421
  320.9 9.1 %collective-permute-done.39 = bf16[288,1152]{1,0:T(8,128)(2,1)} collective-permute-done((bf16[288,1152]{1,0:T(8,128)(2,1)S(1)}, bf16[288,1152]{1,0:T(8,128)(2,1)}, u32[]{:S(2)}, u32[]{:S(2)}) %collective-permute-start.39) | collective-permute-done | bytes 663584 | tf_op jit(solution)/shard_map/ppermute | solution.py:421
  333.3 11.0 %collective-permute-done.22 = bf16[288,1152]{1,0:T(8,128)(2,1)} collective-permute-done((bf16[288,1152]{1,0:T(8,128)(2,1)}, bf16[288,1152]{1,0:T(8,128)(2,1)}, u32[]{:S(2)}, u32[]{:S(2)}) %collective-permute-start.22) | collective-permute-done | bytes 663584 | tf_op jit(solution)/shard_map/ppermute | solution.py:421
  354.0 29.4 %collective-permute-done.23 = bf16[288,1152]{1,0:T(8,128)(2,1)} collective-permute-done((bf16[288,1152]{1,0:T(8,128)(2,1)}, bf16[288,1152]{1,0:T(8,128)(2,1)}, u32[]{:S(2)}, u32[]{:S(2)}) %collective-permute-start.23) | collective-permute-done | bytes 663584 | tf_op jit(solution)/shard_map/ppermute | solution.py:421
  384.9 3.9 collective-permute-start.24
  396.1 7.4 %collective-permute-done.24 = bf16[288,1152]{1,0:T(8,128)(2,1)S(1)} collective-permute-done((bf16[288,1152]{1,0:T(8,128)(2,1)S(1)}, bf16[288,1152]{1,0:T(8,128)(2,1)S(1)}, u32[]{:S(2)}, u32[]{:S(2)}) %collective-permute-start.24) | collective-permute-done | bytes 663584 | tf_op jit(solution)/shard_map/ppermute | solution.py:421
  405.5 4.6 %fusion.1 = f32[1152,1152]{1,0:T(8,128)} fusion(bf16[576,1152]{1,0:T(8,128)(2,1)} %collective-permute-done.35, bf16[576,1152]{1,0:T(8,128)(2,1)S(1)} %maximum_select_fusion.4, pred[]{:T(512)S(6)} %eq.48), kind=kLoop, calls=%fused_computation.3 | loop fusion | flops 13271040 | bytes 7962625 | tf_op jit(solution)/shard_map/convert_element_type | solution.py:741
  410.2 4.6 %fusion.2 = f32[1152,1152]{1,0:T(8,128)} fusion(bf16[576,1152]{1,0:T(8,128)(2,1)} %collective-permute-done.40, bf16[576,1152]{1,0:T(8,128)(2,1)S(1)} %maximum_select_fusion.5, pred[]{:T(512)S(6)} %eq.47), kind=kLoop, calls=%fused_computation.5 | loop fusion | flops 13271040 | bytes 7962625 | tf_op jit(solution)/shard_map/convert_element_type | solution.py:743
  414.8 19.3 %collective-permute-done.25 = bf16[576,1152]{1,0:T(8,128)(2,1)S(1)} collective-permute-done((bf16[576,1152]{1,0:T(8,128)(2,1)S(1)}, bf16[576,1152]{1,0:T(8,128)(2,1)S(1)}, u32[]{:S(2)}, u32[]{:S(2)}) %collective-permute-start.25) | collective-permute-done | bytes 1327136 | tf_op jit(solution)/shard_map/ppermute | solution.py:421
  434.8 3.7 slice_bitcast_fusion
  438.5 3.0 copy.51
  441.5 3.0 copy.52
  444.6 3.0 copy.53
  (218 shorter events, 105.6 us)
Async XLA Ops:
  7.3 339.9 %all-gather.2.cloned.1.call-start = ((), (), s32[]{:S(2)}) async-start(), calls=%async_computation | async-start | bytes 1216512 | tf_op jit(solution)/shard_map/all_gather | solution.py:680
  39.4 17.4 %collective-permute-start.1 = (bf16[256,1152]{1,0:T(8,128)(2,1)}, bf16[256,1152]{1,0:T(8,128)(2,1)S(1)}, u32[]{:S(2)}, u32[]{:S(2)}) collective-permute-start(bf16[256,1152]{1,0:T(8,128)(2,1)} %get-tuple-element.47.refs_0_), channel_id=1, source_target_pairs={{0,2},{1,3},{2,0},{3,1},{4,6},{5,7},{6,4},{7,5},{8,10},{9,11},{10,... | collective-permute-start | bytes 1769480 | tf_op jit(solution)/shard_map/ppermute | solution.py:421
  42.8 25.8 %collective-permute-start.4 = (bf16[256,1152]{1,0:T(8,128)(2,1)S(1)}, bf16[256,1152]{1,0:T(8,128)(2,1)S(1)}, u32[]{:S(2)}, u32[]{:S(2)}) collective-permute-start(bf16[256,1152]{1,0:T(8,128)(2,1)S(1)} %convolution_convert_fusion.1.refs_4_.cotangent_ref), channel_id=1, source_target_pairs={{0,2},{1,3},{2,0},{3,1},{4,6},{5,7},{6,4},{7,5},{8,10},{9,11},{10,... | collective-permute-start | bytes 1769480 | tf_op jit(solution)/shard_map/ppermute | solution.py:421
  42.9 35.3 %collective-permute-start = (bf16[256,1152]{1,0:T(8,128)(2,1)}, bf16[256,1152]{1,0:T(8,128)(2,1)S(1)}, u32[]{:S(2)}, u32[]{:S(2)}) collective-permute-start(bf16[256,1152]{1,0:T(8,128)(2,1)} %get-tuple-element.47.refs_0_), channel_id=1, source_target_pairs={{0,1},{1,0},{2,3},{3,2},{4,5},{5,4},{6,7},{7,6},{8,9},{9,8},{10,11... | collective-permute-start | bytes 1769480 | tf_op jit(solution)/shard_map/ppermute | solution.py:421
  43.0 37.1 %collective-permute-start.3 = (bf16[256,1152]{1,0:T(8,128)(2,1)S(1)}, bf16[256,1152]{1,0:T(8,128)(2,1)}, u32[]{:S(2)}, u32[]{:S(2)}) collective-permute-start(bf16[256,1152]{1,0:T(8,128)(2,1)S(1)} %convolution_convert_fusion.1.refs_4_.cotangent_ref), channel_id=1, source_target_pairs={{0,1},{1,0},{2,3},{3,2},{4,5},{5,4},{6,7},{7,6},{8,9},{9,8},{10,11... | collective-permute-start | bytes 1769480 | tf_op jit(solution)/shard_map/ppermute | solution.py:421
  56.8 23.2 %collective-permute-start.2 = (bf16[256,1152]{1,0:T(8,128)(2,1)S(1)}, bf16[256,1152]{1,0:T(8,128)(2,1)}, u32[]{:S(2)}, u32[]{:S(2)}) collective-permute-start(bf16[256,1152]{1,0:T(8,128)(2,1)S(1)} %collective-permute-done.1.refs_2_), channel_id=1, source_target_pairs={{0,1},{1,0},{2,3},{3,2},{4,5},{5,4},{6,7},{7,6},{8,9},{9,8},{10,11... | collective-permute-start | bytes 1769480 | tf_op jit(solution)/shard_map/ppermute | solution.py:421
  69.6 132.9 %collective-permute-start.18 = (bf16[256,384]{1,0:T(8,128)(2,1)}, bf16[256,384]{1,0:T(8,128)(2,1)}, u32[]{:S(2)}, u32[]{:S(2)}) collective-permute-start(bf16[256,384]{1,0:T(8,128)(2,1)} %get-tuple-element.147), channel_id=1, source_target_pairs={{0,1},{1,0},{2,3},{3,2},{4,5},{5,4},{6,7},{7,6},{8,9},{9,8},{10,11... | collective-permute-start | bytes 589832 | tf_op jit(solution)/shard_map/ppermute | solution.py:421
  78.2 129.1 %collective-permute-start.19 = (bf16[256,384]{1,0:T(8,128)(2,1)}, bf16[256,384]{1,0:T(8,128)(2,1)}, u32[]{:S(2)}, u32[]{:S(2)}) collective-permute-start(bf16[256,384]{1,0:T(8,128)(2,1)} %get-tuple-element.146), channel_id=1, source_target_pairs={{0,2},{1,3},{2,0},{3,1},{4,6},{5,7},{6,4},{7,5},{8,10},{9,11},{10,... | collective-permute-start | bytes 589832 | tf_op jit(solution)/shard_map/ppermute | solution.py:421
  110.9 57.2 %collective-permute-start.31 = (bf16[576,1152]{1,0:T(8,128)(2,1)}, bf16[576,1152]{1,0:T(8,128)(2,1)}, u32[]{:S(2)}, u32[]{:S(2)}) collective-permute-start(bf16[576,1152]{1,0:T(8,128)(2,1)} %constant_dynamic-slice_fusion.3), channel_id=1, source_target_pairs={{0,8},{4,12},{8,0},{12,4},{16,24},{20,28},{24,16},{28,20},{1,9},{5... | collective-permute-start | bytes 3981320 | tf_op jit(solution)/shard_map/ppermute | solution.py:421
  113.7 72.4 %collective-permute-start.36 = (bf16[576,1152]{1,0:T(8,128)(2,1)}, bf16[576,1152]{1,0:T(8,128)(2,1)}, u32[]{:S(2)}, u32[]{:S(2)}) collective-permute-start(bf16[576,1152]{1,0:T(8,128)(2,1)} %constant_dynamic-slice_fusion.1), channel_id=1, source_target_pairs={{0,4},{4,0},{8,12},{12,8},{16,20},{20,16},{24,28},{28,24},{1,5},{5... | collective-permute-start | bytes 3981320 | tf_op jit(solution)/shard_map/ppermute | solution.py:421
  166.3 43.9 %collective-permute-start.16 = (bf16[256,1152]{1,0:T(8,128)(2,1)}, bf16[256,1152]{1,0:T(8,128)(2,1)S(1)}, u32[]{:S(2)}, u32[]{:S(2)}) collective-permute-start(bf16[256,1152]{1,0:T(8,128)(2,1)} %get-tuple-element.56.branch_ref.refs_5_), channel_id=1, source_target_pairs={{0,2},{1,3},{2,0},{3,1},{4,6},{5,7},{6,4},{7,5},{8,10},{9,11},{10,... | collective-permute-start | bytes 1769480 | tf_op jit(solution)/shard_map/ppermute | solution.py:421
  168.1 16.3 %collective-permute-start.27 = (f32[4,5824]{1,0:T(4,128)S(1)}, f32[4,5824]{1,0:T(4,128)S(1)}, u32[]{:S(2)}, u32[]{:S(2)}) collective-permute-start(f32[4,5824]{1,0:T(4,128)S(1)} %fusion.35), channel_id=1, source_target_pairs={{0,2},{1,3},{2,0},{3,1},{4,6},{5,7},{6,4},{7,5},{8,10},{9,11},{10,... | collective-permute-start | bytes 279560 | tf_op jit(solution)/shard_map/ppermute | solution.py:421
  184.4 27.7 %collective-permute-start.32 = (bf16[288,1152]{1,0:T(8,128)(2,1)S(1)}, bf16[288,1152]{1,0:T(8,128)(2,1)S(1)}, u32[]{:S(2)}, u32[]{:S(2)}) collective-permute-start(bf16[288,1152]{1,0:T(8,128)(2,1)S(1)} %constant_dynamic-slice_fusion.2), channel_id=1, source_target_pairs={{0,4},{4,0},{8,12},{12,8},{16,20},{20,16},{24,28},{28,24},{1,5},{5... | collective-permute-start | bytes 1990664 | tf_op jit(solution)/shard_map/ppermute | solution.py:421
  186.1 15.8 %collective-permute-start.28 = (f32[6976]{0:T(1024)S(1)}, f32[6976]{0:T(1024)S(1)}, u32[]{:S(2)}, u32[]{:S(2)}) collective-permute-start(f32[6976]{0:T(1024)S(1)} %pad_maximum_fusion.2), channel_id=1, source_target_pairs={{0,4},{4,0},{8,12},{12,8},{16,20},{20,16},{24,28},{28,24},{1,5},{5... | collective-permute-start | bytes 83720 | tf_op jit(solution)/shard_map/ppermute | solution.py:421
  205.9 19.1 %collective-permute-start.37 = (bf16[288,1152]{1,0:T(8,128)(2,1)S(1)}, bf16[288,1152]{1,0:T(8,128)(2,1)S(1)}, u32[]{:S(2)}, u32[]{:S(2)}) collective-permute-start(bf16[288,1152]{1,0:T(8,128)(2,1)S(1)} %constant_dynamic-slice_fusion), channel_id=1, source_target_pairs={{0,8},{4,12},{8,0},{12,4},{16,24},{20,28},{24,16},{28,20},{1,9},{5... | collective-permute-start | bytes 1990664 | tf_op jit(solution)/shard_map/ppermute | solution.py:421
  207.4 42.3 %collective-permute-start.15 = (bf16[256,1152]{1,0:T(8,128)(2,1)S(1)}, bf16[256,1152]{1,0:T(8,128)(2,1)}, u32[]{:S(2)}, u32[]{:S(2)}) collective-permute-start(bf16[256,1152]{1,0:T(8,128)(2,1)S(1)} %copy-done.17), channel_id=1, source_target_pairs={{0,1},{1,0},{2,3},{3,2},{4,5},{5,4},{6,7},{7,6},{8,9},{9,8},{10,11... | collective-permute-start | bytes 1769480 | tf_op jit(solution)/shard_map/ppermute | solution.py:421
  212.1 38.1 %collective-permute-start.17 = (bf16[256,1152]{1,0:T(8,128)(2,1)S(1)}, bf16[256,1152]{1,0:T(8,128)(2,1)S(1)}, u32[]{:S(2)}, u32[]{:S(2)}) collective-permute-start(bf16[256,1152]{1,0:T(8,128)(2,1)S(1)} %collective-permute-done.16.refs_7_), channel_id=1, source_target_pairs={{0,1},{1,0},{2,3},{3,2},{4,5},{5,4},{6,7},{7,6},{8,9},{9,8},{10,11... | collective-permute-start | bytes 1769480 | tf_op jit(solution)/shard_map/ppermute | solution.py:421
  213.3 50.7 %collective-permute-start.6 = (bf16[256,1152]{1,0:T(8,128)(2,1)}, bf16[256,1152]{1,0:T(8,128)(2,1)S(1)}, u32[]{:S(2)}, u32[]{:S(2)}) collective-permute-start(bf16[256,1152]{1,0:T(8,128)(2,1)} %get-tuple-element.49), channel_id=1, source_target_pairs={{0,1},{1,0},{2,3},{3,2},{4,5},{5,4},{6,7},{7,6},{8,9},{9,8},{10,11... | collective-permute-start | bytes 1769480 | tf_op jit(solution)/shard_map/ppermute | solution.py:421
  223.2 42.3 %collective-permute-start.8 = (bf16[256,1152]{1,0:T(8,128)(2,1)S(1)}, bf16[256,1152]{1,0:T(8,128)(2,1)}, u32[]{:S(2)}, u32[]{:S(2)}) collective-permute-start(bf16[256,1152]{1,0:T(8,128)(2,1)S(1)} %add_convert_fusion.11), channel_id=1, source_target_pairs={{0,2},{1,3},{2,0},{3,1},{4,6},{5,7},{6,4},{7,5},{8,10},{9,11},{10,... | collective-permute-start | bytes 1769480 | tf_op jit(solution)/shard_map/ppermute | solution.py:421
  225.0 22.2 %collective-permute-start.14 = (bf16[256,896]{1,0:T(8,128)(2,1)S(1)}, bf16[256,896]{1,0:T(8,128)(2,1)S(1)}, u32[]{:S(2)}, u32[]{:S(2)}) collective-permute-start(bf16[256,896]{1,0:T(8,128)(2,1)S(1)} %get-tuple-element.138), channel_id=1, source_target_pairs={{0,3},{1,2},{2,1},{3,0},{4,7},{5,6},{6,5},{7,4},{8,11},{9,10},{10,... | collective-permute-start | bytes 1376264 | tf_op jit(solution)/shard_map/ppermute | solution.py:421
  247.3 20.8 %collective-permute-start.30 = (f32[6976]{0:T(1024)S(1)}, f32[6976]{0:T(1024)S(1)}, u32[]{:S(2)}, u32[]{:S(2)}) collective-permute-start(f32[6976]{0:T(1024)S(1)} %add.178), channel_id=1, source_target_pairs={{0,16},{4,20},{8,24},{12,28},{16,0},{20,4},{24,8},{28,12},{1,17},{... | collective-permute-start | bytes 83720 | tf_op jit(solution)/shard_map/ppermute | solution.py:421
  249.8 47.0 %collective-permute-start.33 = (bf16[288,1152]{1,0:T(8,128)(2,1)S(1)}, bf16[288,1152]{1,0:T(8,128)(2,1)S(1)}, u32[]{:S(2)}, u32[]{:S(2)}) collective-permute-start(bf16[288,1152]{1,0:T(8,128)(2,1)S(1)} %add_convert_fusion.6), channel_id=1, source_target_pairs={{0,16},{4,20},{8,24},{12,28},{16,0},{20,4},{24,8},{28,12},{1,17},{... | collective-permute-start | bytes 1990664 | tf_op jit(solution)/shard_map/ppermute | solution.py:421
  251.0 59.7 %collective-permute-start.38 = (bf16[288,1152]{1,0:T(8,128)(2,1)S(1)}, bf16[288,1152]{1,0:T(8,128)(2,1)}, u32[]{:S(2)}, u32[]{:S(2)}) collective-permute-start(bf16[288,1152]{1,0:T(8,128)(2,1)S(1)} %add_convert_fusion.4), channel_id=1, source_target_pairs={{0,16},{4,20},{8,24},{12,28},{16,0},{20,4},{24,8},{28,12},{1,17},{... | collective-permute-start | bytes 1990664 | tf_op jit(solution)/shard_map/ppermute | solution.py:421
  264.0 48.1 %collective-permute-start.21 = (bf16[576,1152]{1,0:T(8,128)(2,1)S(1)}, bf16[576,1152]{1,0:T(8,128)(2,1)S(1)}, u32[]{:S(2)}, u32[]{:S(2)}) collective-permute-start(bf16[576,1152]{1,0:T(8,128)(2,1)S(1)} %constant_dynamic-slice_fusion.7), channel_id=1, source_target_pairs={{0,4},{4,0},{8,12},{12,8},{16,20},{20,16},{24,28},{28,24},{1,5},{5... | collective-permute-start | bytes 3981320 | tf_op jit(solution)/shard_map/ppermute | solution.py:421
  297.0 21.7 %collective-permute-start.34 = (bf16[288,1152]{1,0:T(8,128)(2,1)S(1)}, bf16[288,1152]{1,0:T(8,128)(2,1)}, u32[]{:S(2)}, u32[]{:S(2)}) collective-permute-start(bf16[288,1152]{1,0:T(8,128)(2,1)S(1)} %add_convert_fusion.5), channel_id=1, source_target_pairs={{0,4},{4,0},{8,12},{12,8},{16,20},{20,16},{24,28},{28,24},{1,5},{5... | collective-permute-start | bytes 1990664 | tf_op jit(solution)/shard_map/ppermute | solution.py:421
  312.0 18.0 %collective-permute-start.39 = (bf16[288,1152]{1,0:T(8,128)(2,1)S(1)}, bf16[288,1152]{1,0:T(8,128)(2,1)}, u32[]{:S(2)}, u32[]{:S(2)}) collective-permute-start(bf16[288,1152]{1,0:T(8,128)(2,1)S(1)} %add_convert_fusion.3), channel_id=1, source_target_pairs={{0,8},{4,12},{8,0},{12,4},{16,24},{20,28},{24,16},{28,20},{1,9},{5... | collective-permute-start | bytes 1990664 | tf_op jit(solution)/shard_map/ppermute | solution.py:421
  314.8 29.4 %collective-permute-start.22 = (bf16[288,1152]{1,0:T(8,128)(2,1)}, bf16[288,1152]{1,0:T(8,128)(2,1)}, u32[]{:S(2)}, u32[]{:S(2)}) collective-permute-start(bf16[288,1152]{1,0:T(8,128)(2,1)} %constant_dynamic-slice_fusion.6), channel_id=1, source_target_pairs={{0,8},{4,12},{8,0},{12,4},{16,24},{20,28},{24,16},{28,20},{1,9},{5... | collective-permute-start | bytes 1990664 | tf_op jit(solution)/shard_map/ppermute | solution.py:421
  320.4 85.1 %collective-permute-start.35 = (bf16[576,1152]{1,0:T(8,128)(2,1)S(1)}, bf16[576,1152]{1,0:T(8,128)(2,1)}, u32[]{:S(2)}, u32[]{:S(2)}) collective-permute-start(bf16[576,1152]{1,0:T(8,128)(2,1)S(1)} %maximum_select_fusion.4), channel_id=1, source_target_pairs={{0,8},{4,12},{8,0},{12,4},{16,24},{20,28},{24,16},{28,20},{1,9},{5... | collective-permute-start | bytes 3981320 | tf_op jit(solution)/shard_map/ppermute | solution.py:421
  331.7 78.5 %collective-permute-start.40 = (bf16[576,1152]{1,0:T(8,128)(2,1)S(1)}, bf16[576,1152]{1,0:T(8,128)(2,1)}, u32[]{:S(2)}, u32[]{:S(2)}) collective-permute-start(bf16[576,1152]{1,0:T(8,128)(2,1)S(1)} %maximum_select_fusion.5), channel_id=1, source_target_pairs={{0,4},{4,0},{8,12},{12,8},{16,20},{20,16},{24,28},{28,24},{1,5},{5... | collective-permute-start | bytes 3981320 | tf_op jit(solution)/shard_map/ppermute | solution.py:421
  346.3 37.1 %collective-permute-start.23 = (bf16[288,1152]{1,0:T(8,128)(2,1)}, bf16[288,1152]{1,0:T(8,128)(2,1)}, u32[]{:S(2)}, u32[]{:S(2)}) collective-permute-start(bf16[288,1152]{1,0:T(8,128)(2,1)} %add_convert_fusion.8), channel_id=1, source_target_pairs={{0,16},{4,20},{8,24},{12,28},{16,0},{20,4},{24,8},{28,12},{1,17},{... | collective-permute-start | bytes 1990664 | tf_op jit(solution)/shard_map/ppermute | solution.py:421
  384.9 18.6 %collective-permute-start.24 = (bf16[288,1152]{1,0:T(8,128)(2,1)S(1)}, bf16[288,1152]{1,0:T(8,128)(2,1)S(1)}, u32[]{:S(2)}, u32[]{:S(2)}) collective-permute-start(bf16[288,1152]{1,0:T(8,128)(2,1)S(1)} %add_convert_fusion.7), channel_id=1, source_target_pairs={{0,8},{4,12},{8,0},{12,4},{16,24},{20,28},{24,16},{28,20},{1,9},{5... | collective-permute-start | bytes 1990664 | tf_op jit(solution)/shard_map/ppermute | solution.py:421
  403.9 30.1 %collective-permute-start.25 = (bf16[576,1152]{1,0:T(8,128)(2,1)S(1)}, bf16[576,1152]{1,0:T(8,128)(2,1)S(1)}, u32[]{:S(2)}, u32[]{:S(2)}) collective-permute-start(bf16[576,1152]{1,0:T(8,128)(2,1)S(1)} %maximum_select_fusion.3), channel_id=1, source_target_pairs={{0,4},{4,0},{8,12},{12,8},{16,20},{20,16},{24,28},{28,24},{1,5},{5... | collective-permute-start | bytes 3981320 | tf_op jit(solution)/shard_map/ppermute | solution.py:421
  (47 other events, 501.7 us)
Sparse Core Ops, SparseCore 0:
  166.2 54.8 all-gather.1
